TPU v7x, 128 devices: a whole 4x4x4 slice. The times are simulated.
128 devices in a mesh: ctx: 32 (over y, z, core), head: 4 (over x).
Axes of the slice: x: 4, y: 4, z: 4, core: 2. Of those that a mesh axis runs over, the one named last changes fastest.
Arguments:
- query_latent: bfloat16 [4096, 128, 576], P('ctx', 'head'), may hold values from -80 to 80
- d_out: bfloat16 [4096, 128, 512], P('ctx', 'head'), may hold values from -6 to 6
- latent: bfloat16 [65536, 576], P('ctx'), may hold values from -20 to 20
- index_query: bfloat16 [4096, 64, 128], P('ctx', 'head'), may hold values from -8 to 8
- index_weight: float32 [4096, 64], P('ctx', 'head'), may hold values from -3 to 3
- index_key: bfloat16 [65536, 128], P('ctx'), may hold values from -6 to 6
- kl_scale: float32 [4096], P('ctx'), may hold values from 16 to 64
- history: int32 [64, 14], P('ctx'), may hold values from 32 to 959, as said below
- diag_block: int32 [64], P('ctx'), may hold values from 960 to 1023, as said below
Outputs:
- d_query: bfloat16 [4096, 128, 576], P('ctx', 'head')
- d_latent: bfloat16 [65536, 576], P('ctx')
- d_index_query: bfloat16 [4096, 64, 128], P('ctx', 'head')
- d_index_weight: float32 [4096, 64], P('ctx', 'head')
- d_index_key: bfloat16 [65536, 128], P('ctx')
Inputs may be any that keep to these rules, and one draw needn't show every extreme that they name: `history`: only blocks of ctx shards 1 to 29. Within the lists of one ctx shard's 2 query blocks no block appears twice and no ctx shard's blocks appear more than 2 times; some shard's appear exactly 2 times. `diag_block`: all query blocks together name each of the last 64 blocks once.
All inputs are finite; a program needn't handle non-finite values.
Results may differ from a plain program's by a relative error of at most 0.0051.
Values may be sent and summed in bfloat16 or wider, within the bound.
A program may use at most 192 MiB of HBM per device.

v0:
```python
from functools import partial

import jax
import jax.numpy as jnp
from jax import lax
from jax.sharding import PartitionSpec as P

score_scale = 192.0 ** (-0.5)


def silu_slope(values):
    sig_vals = jax.nn.sigmoid(values)
    return sig_vals * (1.0 + values * (1.0 - sig_vals))


def visible_mask(row_count, rows_per_query, key_count, block_size):
    query_pos = lax.broadcasted_iota(jnp.int32, (row_count, key_count), 0) // rows_per_query
    key_pos = lax.broadcasted_iota(jnp.int32, (row_count, key_count), 1) - (key_count - block_size)
    return key_pos <= query_pos


def main_block(block_items):
    q_rows, g_rows, lat_keys, iq_rows, iw_rows, idx_keys = block_items
    block_size, head_count, full_width = q_rows.shape
    value_width = g_rows.shape[2]
    key_count = lat_keys.shape[0]
    idx_count, key_width = (iq_rows.shape[1], iq_rows.shape[2])
    q_flat = q_rows.reshape(block_size * head_count, full_width)
    g_flat = g_rows.reshape(block_size * head_count, value_width)
    visible = visible_mask(block_size * head_count, head_count, key_count, block_size)
    scores = (
        jnp.einsum("rd,td->rt", q_flat, lat_keys, preferred_element_type=jnp.float32) * score_scale
    )
    scores = jnp.where(visible, scores, -jnp.inf)
    row_top = jnp.max(scores, axis=1, keepdims=True)
    row_exp = jnp.exp(scores - row_top)
    prob_rows = row_exp / jnp.sum(row_exp, axis=1, keepdims=True)
    probs_low = prob_rows.astype(jnp.bfloat16)
    d_probs = jnp.einsum(
        "rd,td->rt", g_flat, lat_keys[:, :value_width], preferred_element_type=jnp.float32
    )
    row_delta = jnp.sum(prob_rows * d_probs, axis=1, keepdims=True)
    d_scores = (prob_rows * (d_probs - row_delta) * score_scale).astype(jnp.bfloat16)
    d_query = jnp.dot(d_scores, lat_keys, preferred_element_type=jnp.float32).astype(jnp.bfloat16)
    key_grad = jnp.einsum("rt,rd->td", d_scores, q_flat, preferred_element_type=jnp.float32)
    value_grad = jnp.einsum("rt,rd->td", probs_low, g_flat, preferred_element_type=jnp.float32)
    key_grad = key_grad + jnp.pad(value_grad, ((0, 0), (0, full_width - value_width)))
    prob_sum = jnp.sum(prob_rows.reshape(block_size, head_count, key_count), axis=1)
    iq_flat = iq_rows.reshape(block_size * idx_count, key_width)
    logits = jnp.einsum(
        "rd,td->rt", iq_flat, idx_keys, preferred_element_type=jnp.float32
    ) * key_width ** (-0.5)
    gated_vals = jax.nn.silu(logits).reshape(block_size, idx_count, key_count)
    score_part = jnp.sum(iw_rows[:, :, None] * gated_vals, axis=1)
    return (
        d_query.reshape(block_size, head_count, full_width),
        key_grad,
        prob_sum,
        score_part,
        logits,
    )


def index_block(head_total, block_items):
    prob_total, score_total, logits, iq_rows, iw_rows, idx_keys, loss_rows = block_items
    block_size, idx_count, key_width = iq_rows.shape
    key_count = idx_keys.shape[0]
    near_mask = visible_mask(block_size, 1, key_count, block_size)
    masked = jnp.where(near_mask, score_total, -jnp.inf)
    row_peak = jnp.max(masked, axis=1, keepdims=True)
    index_exp = jnp.exp(masked - row_peak)
    index_prob = index_exp / jnp.sum(index_exp, axis=1, keepdims=True)
    target = prob_total / head_total
    d_score = loss_rows[:, None] * (index_prob - target)
    logit_cube = logits.reshape(block_size, idx_count, key_count)
    d_weight = jnp.sum(d_score[:, None, :] * jax.nn.silu(logit_cube), axis=2)
    d_logit = (
        d_score[:, None, :] * iw_rows[:, :, None] * silu_slope(logit_cube) * key_width ** (-0.5)
    ).astype(jnp.bfloat16)
    d_logit = d_logit.reshape(block_size * idx_count, key_count)
    iq_flat = iq_rows.reshape(block_size * idx_count, key_width)
    d_iq = jnp.dot(d_logit, idx_keys, preferred_element_type=jnp.float32).astype(jnp.bfloat16)
    ikey_grad = jnp.einsum("rt,rd->td", d_logit, iq_flat, preferred_element_type=jnp.float32)
    return (d_iq.reshape(block_size, idx_count, key_width), d_weight, ikey_grad)


def shards(
    query_latent, d_out, latent, index_query, index_weight, index_key, kl_scale, history, diag_block
):
    q_dev, head_count, full_width = query_latent.shape
    value_width = d_out.shape[2]
    idx_count, key_width = (index_query.shape[1], index_query.shape[2])
    q_blocks, hist_count = history.shape
    block_size = q_dev // q_blocks
    context_dev = latent.shape[0]
    blk_dev = context_dev // block_size
    ctx_count = lax.axis_size("ctx")
    head_groups = lax.axis_size("head")
    pick_count = hist_count + 2
    all_blocks = blk_dev * ctx_count
    slab_blocks = q_blocks * ctx_count
    hist_owners = (all_blocks - slab_blocks) // blk_dev
    hist_cap = max(2, (q_blocks * hist_count + hist_owners - 2) // (hist_owners - 1))
    owner_cap = max(hist_cap, q_blocks)
    wanted = jnp.concatenate([history.reshape(-1), diag_block])
    wanted = jnp.concatenate([wanted, jnp.zeros((1,), jnp.int32)])
    request_count = wanted.shape[0]
    owner_of = wanted // blk_dev
    local_id = wanted % blk_dev
    order_iota = jnp.arange(request_count)
    earlier = (order_iota[None, :] < order_iota[:, None]) & (owner_of[None, :] == owner_of[:, None])
    slot_rank = jnp.sum(earlier.astype(jnp.int32), axis=1)
    slot_of = owner_of * owner_cap + slot_rank
    slot_total = ctx_count * owner_cap
    slot_hits = slot_of[:, None] == jnp.arange(slot_total)[None, :]
    ask_table = jnp.sum(jnp.where(slot_hits, local_id[:, None] + 1, 0), axis=0) - 1
    asked_ids = lax.all_to_all(
        ask_table.reshape(ctx_count, owner_cap), "ctx", split_axis=0, concat_axis=0, tiled=True
    )
    source_id = jnp.clip(asked_ids, 0, blk_dev - 1)
    lat_local = latent.reshape(blk_dev, block_size, full_width)
    key_local = index_key.reshape(blk_dev, block_size, key_width)
    lat_source, key_source = (lat_local, key_local)
    sent_lat = jnp.take(lat_source, source_id, axis=0)
    sent_key = jnp.take(key_source, source_id, axis=0)
    got_lat, got_key = (
        lax.all_to_all(sent_lat, "ctx", split_axis=0, concat_axis=0, tiled=True),
        lax.all_to_all(sent_key, "ctx", split_axis=0, concat_axis=0, tiled=True),
    )
    lat_slots = got_lat.reshape(slot_total, block_size, full_width)
    key_slots = got_key.reshape(slot_total, block_size, key_width)
    hist_slots = slot_of[: q_blocks * hist_count].reshape(q_blocks, hist_count)
    diag_slots = slot_of[q_blocks * hist_count : q_blocks * hist_count + q_blocks]
    sink_slot = slot_of[request_count - 1]
    lat_pool, key_pool = (lat_slots, key_slots)
    pool_size = lat_pool.shape[0]
    sink_col = jnp.zeros((q_blocks, 1), jnp.int32) + sink_slot
    block_slots = jnp.concatenate([sink_col, hist_slots, diag_slots[:, None]], axis=1)
    key_count = pick_count * block_size
    lat_keys = jnp.take(lat_pool, block_slots, axis=0).reshape(q_blocks, key_count, full_width)
    idx_keys = jnp.take(key_pool, block_slots, axis=0).reshape(q_blocks, key_count, key_width)
    q_blocked = query_latent.reshape(q_blocks, block_size, head_count, full_width)
    g_blocked = d_out.reshape(q_blocks, block_size, head_count, value_width)
    iq_blocked = index_query.reshape(q_blocks, block_size, idx_count, key_width)
    iw_blocked = index_weight.reshape(q_blocks, block_size, idx_count)
    loss_blocked = kl_scale.reshape(q_blocks, block_size)
    d_query, key_grad, prob_sum, score_part, logits = lax.map(
        main_block, (q_blocked, g_blocked, lat_keys, iq_blocked, iw_blocked, idx_keys)
    )
    prob_total, score_total = lax.psum((prob_sum, score_part), "head")
    head_total = head_count * head_groups
    d_iq, d_weight, ikey_grad = lax.map(
        partial(index_block, head_total),
        (prob_total, score_total, logits, iq_blocked, iw_blocked, idx_keys, loss_blocked),
    )
    flat_slots = block_slots.reshape(-1)
    grad_pool = (
        jnp.zeros((pool_size, block_size, full_width), jnp.float32)
        .at[flat_slots]
        .add(key_grad.reshape(q_blocks * pick_count, block_size, full_width))
    )
    ikey_pool = (
        jnp.zeros((pool_size, block_size, key_width), jnp.float32)
        .at[flat_slots]
        .add(ikey_grad.reshape(q_blocks * pick_count, block_size, key_width))
    )
    grad_slots = grad_pool.reshape(ctx_count, owner_cap, block_size, full_width)
    ikey_slots = ikey_pool.reshape(ctx_count, owner_cap, block_size, key_width)
    flat_source = source_id.reshape(-1)
    back_lat, back_key = (
        lax.all_to_all(grad_slots, "ctx", split_axis=0, concat_axis=0, tiled=True),
        lax.all_to_all(ikey_slots, "ctx", split_axis=0, concat_axis=0, tiled=True),
    )
    owned_lat = (
        jnp.zeros((blk_dev, block_size, full_width), jnp.float32)
        .at[flat_source]
        .add(back_lat.reshape(slot_total, block_size, full_width))
    )
    owned_key = (
        jnp.zeros((blk_dev, block_size, key_width), jnp.float32)
        .at[flat_source]
        .add(back_key.reshape(slot_total, block_size, key_width))
    )
    owned_lat, owned_key = lax.psum((owned_lat, owned_key), "head")
    d_latent = owned_lat.reshape(context_dev, full_width).astype(jnp.bfloat16)
    d_ikey = owned_key.reshape(context_dev, key_width).astype(jnp.bfloat16)
    return (
        d_query.reshape(q_dev, head_count, full_width),
        d_latent,
        d_iq.reshape(q_dev, idx_count, key_width),
        d_weight.reshape(q_dev, idx_count),
        d_ikey,
    )


def solution(mesh):
    in_specs = (
        P("ctx", "head", None),
        P("ctx", "head", None),
        P("ctx", None),
        P("ctx", "head", None),
        P("ctx", "head"),
        P("ctx", None),
        P("ctx"),
        P("ctx", None),
        P("ctx"),
    )
    out_specs = (
        P("ctx", "head", None),
        P("ctx", None),
        P("ctx", "head", None),
        P("ctx", "head"),
        P("ctx", None),
    )
    return jax.shard_map(shards, mesh=mesh, in_specs=in_specs, out_specs=out_specs, check_vma=False)
```

profile of v0, /device:TPU:48, one launch (start us, length us, event | category | flops | bytes accessed | tf_op | source)
XLA Modules:
  0.0 661.0 jit_solution(16072805810531794943)
XLA Ops:
  9.1 12.2 %all_to_all.26 = s32[32,1,2]{2,1,0:T(1,128)S(1)} all-to-all(s32[32,1,2]{2,1,0:T(1,128)S(1)} %bitcast.220), channel_id=1, replica_groups=mesh['ctx'=32,'head'=4] {'ctx'}, dimensions={0} | all-to-all | bytes 512 | tf_op jit(solution)/shard_map/all_to_all | solution.py:117
  24.3 7.5 %all-to-all-start.2 = ((bf16[32,2,64,128]{3,2,1,0:T(8,128)(2,1)}), bf16[32,2,64,128]{3,2,1,0:T(8,128)(2,1)}, u32[]{:S(2)}, u32[]{:S(2)}) async-start(bf16[32,2,64,128]{3,2,1,0:T(8,128)(2,1)} %broadcast_select_fusion.1), calls=%async_computation.2 | async-start | bytes 2097152 | tf_op jit(solution)/shard_map/all_to_all | solution.py:128
  38.4 5.5 broadcast_select_fusion
  45.6 7.9 %all-to-all-start.1 = ((bf16[32,2,64,576]{3,2,1,0:T(8,128)(2,1)}), bf16[32,2,64,576]{3,2,1,0:T(8,128)(2,1)}, u32[]{:S(2)}, u32[]{:S(2)}) async-start(bf16[32,2,64,576]{3,2,1,0:T(8,128)(2,1)} %broadcast_select_fusion), calls=%async_computation.1 | async-start | bytes 10485760 | tf_op jit(solution)/shard_map/all_to_all | solution.py:127
  56.3 8.9 %copy.70 = bf16[128,32,576]{2,1,0:T(8,128)(2,1)} copy(bf16[128,32,576]{0,2,1:T(8,128)(2,1)} %param.13) | data formatting | bytes 9437184 | tf_op args[0]
  68.2 52.5 %all-to-all-done.1 = bf16[32,2,64,576]{3,2,1,0:T(8,128)(2,1)} async-done(((bf16[32,2,64,576]{3,2,1,0:T(8,128)(2,1)}), bf16[32,2,64,576]{3,2,1,0:T(8,128)(2,1)}, u32[]{:S(2)}, u32[]{:S(2)}) %all-to-all-start.1) | async-done | bytes 4718624 | tf_op jit(solution)/shard_map/all_to_all | solution.py:127
  120.7 4.8 gather_fusion.1
  127.6 95.6 %while.36 = (s32[]{:T(128)}, bf16[2,64,32,576]{3,2,1,0:T(8,128)(2,1)}, f32[2,1024,576]{1,2,0:T(8,128)}, f32[2,64,1024]{2,1,0:T(8,128)}, f32[2,64,1024]{2,1,0:T(8...) while((s32[]{:T(128)}, ...), condition=%wide.region_8.9_spmd, body=%wide.region_2.8_spmd.sunk | while | flops 11873627136 | bytes 191797616 | solution.py:147
  142.9 4.2 fusion.76
  147.1 4.7 fusion.77
  162.0 4.2 bitcast_dynamic-update-slice_fusion.7
  166.2 3.9 convolution_convert_fusion.4
  184.5 4.2 fusion.76
  188.8 4.7 fusion.77
  203.6 4.2 bitcast_dynamic-update-slice_fusion.7
  207.8 3.9 convolution_convert_fusion.4
  223.4 45.8 %all-reduce.6.cloned.1.call-done = (f32[2,64,1024]{2,1,0:T(8,128)}, f32[2,64,1024]{2,1,0:T(8,128)}) async-done(((f32[2,64,1024]{2,1,0:T(8,128)}, f32[2,64,1024]{2,1,0:T(8,128)}), (f32[2,64,1024]{2,1,0:T(8,128)}, f32[2,64,1024]{2,1,0:T(8,128)})) %all-reduce.6.cloned.1.call-update) | async-done | bytes 1048592 | tf_op jit(solution)/shard_map/psum | solution.py:150
  269.3 29.3 %while.37 = (s32[]{:T(128)}, bf16[2,64,16,128]{3,2,1,0:T(8,128)(2,1)}, f32[2,64,16]{2,1,0:T(8,128)S(1)}, f32[2,1024,128]{2,1,0:T(8,128)S(1)}, f32[2,64]{1,0:T(2,...) while((s32[]{:T(128)}, ...), condition=%wide.region_18.19_spmd, body=%wide.region_14.18_spmd.sunk | while | flops 555745152 | bytes 39962892 | solution.py:152
  273.3 5.4 fusion.87
  288.0 5.4 fusion.87
  300.2 4.8 scatter_fusion.2
  304.9 7.5 %all-to-all-start.4 = ((f32[32,2,64,128]{3,2,1,0:T(8,128)}), f32[32,2,64,128]{3,2,1,0:T(8,128)S(1)}, u32[]{:S(2)}, u32[]{:S(2)}) async-start(f32[32,2,64,128]{3,2,1,0:T(8,128)} %bitcast.51), calls=%async_computation.4 | async-start | bytes 4194304 | tf_op jit(solution)/shard_map/all_to_all | solution.py:172
  312.4 5.8 copy.81
  318.2 5.1 broadcast_in_dim.193
  323.3 11.6 %scatter_fusion = f32[64,64,576]{2,1,0:T(8,128)} fusion(f32[64,64,576]{2,1,0:T(8,128)} %broadcast_in_dim.193, s32[32]{0:T(128)S(1)} %fusion.26, f32[32,64,576]{2,1,0:T(8,128)} %bitcast.207), kind=kCustom, calls=%fused_computation.4 | custom fusion | flops 1179648 | bytes 14155904 | tf_op jit(solution)/shard_map/scatter-add | solution.py:160
  338.2 9.3 %all-to-all-start.3 = ((f32[32,2,64,576]{3,2,1,0:T(8,128)}), f32[32,2,64,576]{3,2,1,0:T(8,128)}, u32[]{:S(2)}, u32[]{:S(2)}) async-start(f32[32,2,64,576]{3,2,1,0:T(8,128)} %bitcast.198), calls=%async_computation.3 | async-start | bytes 20971520 | tf_op jit(solution)/shard_map/all_to_all | solution.py:171
  347.7 8.6 %copy.84 = bf16[128,32,576]{0,2,1:T(8,128)(2,1)} copy(bf16[128,32,576]{2,1,0:T(8,128)(2,1)} %bitcast.212) | data formatting | bytes 9437184
  357.1 7.0 %scatter_fusion.3 = f32[32,64,128]{2,1,0:T(8,128)S(1)} fusion(f32[32,64,128]{2,1,0:T(8,128)S(1)} %broadcast_in_dim.197, s32[64]{0:T(128)S(1)} %fusion.25, f32[64,64,128]{2,1,0:T(8,128)} %bitcast.211), kind=kCustom, calls=%fused_computation.7 | custom fusion | flops 524288 | bytes 6291712 | tf_op jit(solution)/shard_map/scatter-add | solution.py:182
  364.2 148.6 %all-to-all-done.3 = f32[32,2,64,576]{3,2,1,0:T(8,128)} async-done(((f32[32,2,64,576]{3,2,1,0:T(8,128)}), f32[32,2,64,576]{3,2,1,0:T(8,128)}, u32[]{:S(2)}, u32[]{:S(2)}) %all-to-all-start.3) | async-done | bytes 9437216 | tf_op jit(solution)/shard_map/all_to_all | solution.py:171
  515.8 21.2 %scatter_fusion.1 = f32[32,64,576]{2,1,0:T(8,128)} fusion(f32[32,64,576]{2,1,0:T(8,128)} %broadcast_in_dim.192, s32[64]{0:T(128)S(1)} %fusion.25, f32[64,64,576]{2,1,0:T(8,128)} %bitcast.46), kind=kCustom, calls=%fused_computation.5 | custom fusion | flops 2359296 | bytes 28311808 | tf_op jit(solution)/shard_map/scatter-add | solution.py:177
  537.0 112.4 %all-reduce.7 = (bf16[32,64,576]{2,1,0:T(8,128)(2,1)}, bf16[32,64,128]{2,1,0:T(8,128)(2,1)}) all-reduce(f32[32,64,576]{2,1,0:T(8,128)} %scatter_fusion.1, f32[32,64,128]{2,1,0:T(8,128)S(1)} %scatter_fusion.3), channel_id=1, replica_groups=mesh['ctx'=32,'head'=4] {'head'}, use_global_device_ids=true, to_apply=%region_11.12 | all-reduce | flops 1441792 | bytes 8650752 | tf_op jit(solution)/shard_map/psum | solution.py:184
  649.4 4.3 copy.85
  (185 shorter events, 96.8 us)
Async XLA Ops:
  7.2 15.2 %copy-start = (bf16[2048,128]{1,0:T(8,128)(2,1)S(1)}, bf16[2048,128]{1,0:T(8,128)(2,1)}, u32[]{:S(2)}) copy-start(bf16[2048,128]{1,0:T(8,128)(2,1)} %param.18) | copy-start | bytes 1572868
  24.3 21.3 %all-to-all-start.2 = ((bf16[32,2,64,128]{3,2,1,0:T(8,128)(2,1)}), bf16[32,2,64,128]{3,2,1,0:T(8,128)(2,1)}, u32[]{:S(2)}, u32[]{:S(2)}) async-start(bf16[32,2,64,128]{3,2,1,0:T(8,128)(2,1)} %broadcast_select_fusion.1), calls=%async_computation.2 | async-start | bytes 2097152 | tf_op jit(solution)/shard_map/all_to_all | solution.py:128
  43.9 12.3 %copy-start.14 = (f32[128,16]{0,1:T(8,128)S(1)}, f32[128,16]{0,1:T(8,128)}, u32[]{:S(2)}) copy-start(f32[128,16]{0,1:T(8,128)} %param.17) | copy-start | bytes 24580
  45.6 75.1 %all-to-all-start.1 = ((bf16[32,2,64,576]{3,2,1,0:T(8,128)(2,1)}), bf16[32,2,64,576]{3,2,1,0:T(8,128)(2,1)}, u32[]{:S(2)}, u32[]{:S(2)}) async-start(bf16[32,2,64,576]{3,2,1,0:T(8,128)(2,1)} %broadcast_select_fusion), calls=%async_computation.1 | async-start | bytes 10485760 | tf_op jit(solution)/shard_map/all_to_all | solution.py:127
  53.5 215.8 %all-reduce.6.cloned.1.call-start = ((), (), s32[]{:S(2)}) async-start(), calls=%async_computation.5 | async-start | bytes 2097152 | tf_op jit(solution)/shard_map/psum | solution.py:150
  127.5 95.7 %copy-start.18 = (f32[128]{0:T(128)S(1)}, f32[128]{0:T(128)}, u32[]{:S(2)}) copy-start(f32[128]{0:T(128)} %param.19) | copy-start | bytes 1540
  127.6 95.8 %copy-start.15 = (s32[2,16]{1,0:T(2,128)S(1)}, s32[2,16]{1,0:T(2,128)}, u32[]{:S(2)}) copy-start(s32[2,16]{1,0:T(2,128)} %get-tuple-element.462) | copy-start | bytes 388
  139.9 7.2 %copy-start.2 = (bf16[2,1024,576]{2,1,0:T(8,128)(2,1)}, bf16[2,1024,576]{2,1,0:T(8,128)(2,1)S(1)}, u32[]{:S(2)}) copy-start(bf16[2,1024,576]{2,1,0:T(8,128)(2,1)S(1)} %get-tuple-element.682) | copy-start | bytes 7077892 | tf_op jit(solution)/shard_map/while
  151.9 3.9 copy-start.4
  173.2 1.8 copy-start.6
  175.0 3.1 copy-start.9
  175.0 3.1 copy-start.11
  178.1 1.0 copy-start.12
  179.1 2.5 copy-start.3
  181.6 7.2 %copy-start.2 = (bf16[2,1024,576]{2,1,0:T(8,128)(2,1)}, bf16[2,1024,576]{2,1,0:T(8,128)(2,1)S(1)}, u32[]{:S(2)}) copy-start(bf16[2,1024,576]{2,1,0:T(8,128)(2,1)S(1)} %get-tuple-element.682) | copy-start | bytes 7077892 | tf_op jit(solution)/shard_map/while
  193.5 3.9 copy-start.4
  214.8 1.8 copy-start.6
  216.6 3.1 copy-start.9
  216.6 3.1 copy-start.11
  219.8 1.0 copy-start.12
  220.7 2.5 copy-start.3
  278.7 3.5 copy-start.5
  278.8 4.1 copy-start.7
  278.8 4.1 copy-start.16
  293.4 3.5 copy-start.5
  293.5 4.1 copy-start.7
  293.5 4.1 copy-start.16
  304.9 32.0 %all-to-all-start.4 = ((f32[32,2,64,128]{3,2,1,0:T(8,128)}), f32[32,2,64,128]{3,2,1,0:T(8,128)S(1)}, u32[]{:S(2)}, u32[]{:S(2)}) async-start(f32[32,2,64,128]{3,2,1,0:T(8,128)} %bitcast.51), calls=%async_computation.4 | async-start | bytes 4194304 | tf_op jit(solution)/shard_map/all_to_all | solution.py:172
  336.9 1.3 copy-start.8
  336.9 10.7 %copy-start.13 = (s32[32,2]{1,0:T(8,128)S(1)}, s32[32,2]{1,0:T(8,128)}, u32[]{:S(2)}) copy-start(s32[32,2]{1,0:T(8,128)} %get-tuple-element.475) | copy-start | bytes 772
  338.2 174.6 %all-to-all-start.3 = ((f32[32,2,64,576]{3,2,1,0:T(8,128)}), f32[32,2,64,576]{3,2,1,0:T(8,128)}, u32[]{:S(2)}, u32[]{:S(2)}) async-start(f32[32,2,64,576]{3,2,1,0:T(8,128)} %bitcast.198), calls=%async_computation.3 | async-start | bytes 20971520 | tf_op jit(solution)/shard_map/all_to_all | solution.py:171
  515.8 138.0 %copy-start.1 = (bf16[2048,128]{1,0:T(8,128)(2,1)S(1)}, bf16[2048,128]{1,0:T(8,128)(2,1)}, u32[]{:S(2)}) copy-start(bf16[2048,128]{1,0:T(8,128)(2,1)} %param.18) | copy-start | bytes 1572868
  (4 other events, 3.2 us)
Sparse Core Ops, SparseCore 0:
  223.3 45.8 all-reduce.5
where the time goes:
time: 667 us; the launch traced here: 661 us
  waiting for transfers between devices  251 us (38%)
  blocking collectives  125 us (19%)
  other arithmetic  106 us (16%)
  local copies, waits for them, and re-layouts  76.8 us (12%)
  matrix products  43.3 us (6%)
  starting transfers between devices  32.3 us (5%)
  between operations  14.6 us (2%)
  loops' own time  13 us (2%)
    all_to_all x1, waiting for transfers between devices, shards(): lax.all_to_all(grad_slots, 'ctx', split_axis=0, concat_axis=0, tiled=True)  149 us
    psum x1, blocking collectives, shards(): owned_lat, owned_key = lax.psum((owned_lat, owned_key), 'head')  112 us
    all_to_all x1, waiting for transfers between devices, shards(): lax.all_to_all(sent_lat, 'ctx', split_axis=0, concat_axis=0, tiled=True)  52.5 us
    psum x1, waiting for transfers between devices, shards(): prob_total, score_total = lax.psum((prob_sum, score_part), 'head')  45.8 us
    unnamed x18, local copies, waits for them, and re-layouts  26.3 us
    scatter-add x1, other arithmetic, shards(): owned_lat = jnp.zeros((blk_dev, block_size, full_width), jnp.float32).at[...  21.2 us
  transfers between devices with their start and end apart: 5, of which 5 were waited for; matrix products, arithmetic and copies ran while one was open for 10% of the time, Pallas kernels for 0%

commit v1 on v0

v1 whole, which is shorter than its diff:
```python
from functools import partial

import jax
import jax.numpy as jnp
from jax import lax
from jax.experimental import pallas as pl
from jax.experimental.pallas import tpu as pltpu
from jax.sharding import PartitionSpec as P

MESH = pl.DeviceIdType.MESH
f32, bf16, i32 = jnp.float32, jnp.bfloat16, jnp.int32

SCORE_SCALE = 192.0 ** (-0.5)
LOG2E = 1.4426950408889634
BLOCK = 64
SLOTS = 2
LANES = 128


def iota(shape, dim):
    return lax.broadcasted_iota(i32, shape, dim)


def one_hot(index_rows, width):
    wide = jnp.concatenate([index_rows] * (width // LANES), axis=1)
    hit = wide == iota(wide.shape, 1)
    return jnp.where(hit, 1.0, 0.0).astype(bf16)


def slot_rows(ids, sel, n_ctx, quarter):
    @pl.loop(0, n_ctx)
    def _(r):
        for s in range(SLOTS):
            row = jnp.broadcast_to(ids[r, s : s + 1, :], (quarter, LANES))
            start = pl.multiple_of((r * SLOTS + s) * quarter, quarter)
            sel[pl.ds(start, quarter), :] = row * quarter + iota((quarter, LANES), 0)


def greet(n_ctx, n_head, with_ctx):
    me, col = lax.axis_index("ctx"), lax.axis_index("head")
    barrier = pltpu.get_barrier_semaphore()
    count = 0
    if with_ctx:

        @pl.loop(1, n_ctx)
        def _(d):
            pl.semaphore_signal(
                barrier, inc=1, device_id=(lax.rem(me + d, n_ctx), col), device_id_type=MESH
            )

        count += n_ctx - 1
    for d in range(1, n_head):
        pl.semaphore_signal(
            barrier, inc=1, device_id=(me, lax.rem(col + d, n_head)), device_id_type=MESH
        )
    pl.semaphore_wait(barrier, count + n_head - 1)


def ctx_copy(src, dst, send_sem, recv_sem, d, n_ctx):
    me, col = lax.axis_index("ctx"), lax.axis_index("head")
    to = lax.rem(me + d, n_ctx)
    return pltpu.make_async_remote_copy(
        src_ref=src.at[to],
        dst_ref=dst.at[me],
        send_sem=send_sem.at[d],
        recv_sem=recv_sem.at[d],
        device_id=(to, col),
        device_id_type=MESH,
    )


def ctx_arrival(src, dst, send_sem, recv_sem, d, n_ctx):
    me, col = lax.axis_index("ctx"), lax.axis_index("head")
    to = lax.rem(me + d, n_ctx)
    come = lax.rem(me - d + n_ctx, n_ctx)
    return pltpu.make_async_remote_copy(
        src_ref=src.at[to],
        dst_ref=dst.at[come],
        send_sem=send_sem.at[d],
        recv_sem=recv_sem.at[d],
        device_id=(to, col),
        device_id_type=MESH,
    )


def exchange_ctx(src, dst, send_sem, recv_sem, n_ctx):
    @pl.loop(1, n_ctx)
    def _(d):
        ctx_copy(src, dst, send_sem, recv_sem, d, n_ctx).start()


def finish_ctx(src, dst, send_sem, recv_sem, n_ctx):
    @pl.loop(1, n_ctx)
    def _(d):
        arrival = ctx_arrival(src, dst, send_sem, recv_sem, d, n_ctx)
        arrival.wait_recv()
        arrival.wait_send()


def head_copy(src, dst, send_sem, recv_sem, d, n_head):
    me, col = lax.axis_index("ctx"), lax.axis_index("head")
    return pltpu.make_async_remote_copy(
        src_ref=src,
        dst_ref=dst,
        send_sem=send_sem,
        recv_sem=recv_sem,
        device_id=(me, lax.rem(col + d, n_head)),
        device_id_type=MESH,
    )


def gather_kernel(
    n_ctx, n_head, ask, want, lat, key, k_out, ids,
    latq, keyq, sel, send, recv, comp,
    load_sem, ask_send, ask_recv, a_send, a_recv, x_send, x_recv,
):
    me, col = lax.axis_index("ctx"), lax.axis_index("head")
    blocks, quarter, lat_width = latq.shape
    entries = comp.shape[0]
    mine = pl.ds(pl.multiple_of(col * quarter, quarter), quarter)
    load_lat = pltpu.make_async_copy(lat.at[:, mine], latq, load_sem.at[0])
    load_key = pltpu.make_async_copy(key.at[:, mine], keyq, load_sem.at[1])
    load_lat.start()
    load_key.start()
    greet(n_ctx, n_head, True)

    exchange_ctx(ask, ids, ask_send, ask_recv, n_ctx)
    ids[me] = ask[me]
    load_lat.wait()
    load_key.wait()
    finish_ctx(ask, ids, ask_send, ask_recv, n_ctx)
    slot_rows(ids, sel, n_ctx, quarter)

    per = 256 // (SLOTS * quarter)

    @pl.loop(0, n_ctx // per)
    def _(i):
        start = pl.multiple_of(i * 256, 256)
        pick = one_hot(sel[pl.ds(start, 256), :], blocks * quarter)
        lat_rows = jnp.dot(
            pick, latq[...].reshape(blocks * quarter, lat_width), preferred_element_type=f32
        )
        key_rows = jnp.dot(
            pick, keyq[...].reshape(blocks * quarter, LANES), preferred_element_type=f32
        )
        pad = jnp.zeros((256, 640 - lat_width), f32)
        rows = jnp.concatenate([lat_rows, pad, key_rows], axis=1).astype(bf16)
        send[pl.ds(i * per, per)] = rows.reshape(per, SLOTS * quarter, 768)

    exchange_ctx(send, recv, a_send, a_recv, n_ctx)
    recv[me] = send[me]
    finish_ctx(send, recv, a_send, a_recv, n_ctx)

    @pl.loop(0, entries * quarter // 256)
    def _(i):
        start = pl.multiple_of(i * 256, 256)
        pick = one_hot(want[pl.ds(start, 256), :], n_ctx * SLOTS * quarter)
        rows = jnp.dot(
            pick, recv[...].reshape(n_ctx * SLOTS * quarter, 768), preferred_element_type=f32
        ).astype(bf16)
        comp[pl.ds(i * (256 // quarter), 256 // quarter)] = rows.reshape(256 // quarter, quarter, 768)

    def place(d):
        return head_copy(comp, k_out.at[:, col], x_send.at[d], x_recv.at[d], d, n_head)

    for d in range(1, n_head):
        place(d).start()
    k_out[:, col] = comp[...]
    for d in range(1, n_head):
        come = lax.rem(col - d + n_head, n_head)
        arrival = head_copy(comp, k_out.at[:, come], x_send.at[d], x_recv.at[d], d, n_head)
        arrival.wait_recv()
        arrival.wait_send()


def main_kernel(
    n_head, head_total, q_hbm, g_hbm, keys, iq, iw, kl, dq_hbm, diq, dw, tq,
    qbuf, gbuf, dqbuf, kt, acc, ik_acc, logit, ex, exr, dsb, ktb, rsr, ikb, ikr,
    q_sem, g_sem, dq_sem, ex_send, ex_recv, ds_send, ds_recv, rs_send, rs_recv, ik_send, ik_recv,
):
    me, col = lax.axis_index("ctx"), lax.axis_index("head")
    groups, key_count, _ = keys.shape
    lat_width, val_width = qbuf.shape[1], gbuf.shape[1]
    heads = qbuf.shape[0] // (groups * BLOCK)
    idx_heads = iq.shape[0] // (groups * BLOCK)
    span = BLOCK // n_head
    chunk = span * heads
    sub = 256
    idx_scale = LANES ** (-0.5)
    exp_scale = SCORE_SCALE * LOG2E

    def q_load(n):
        rows = pl.ds(pl.multiple_of(n * chunk, chunk), chunk)
        return pltpu.make_async_copy(q_hbm.at[rows], qbuf.at[rows], q_sem.at[n])

    def g_load(n):
        rows = pl.ds(pl.multiple_of(n * chunk, chunk), chunk)
        return pltpu.make_async_copy(g_hbm.at[rows], gbuf.at[rows], g_sem.at[n])

    def dq_store(n):
        rows = pl.ds(pl.multiple_of(n * chunk, chunk), chunk)
        return pltpu.make_async_copy(dqbuf.at[rows], dq_hbm.at[rows], dq_sem.at[n])

    for n in range(groups * n_head):
        q_load(n).start()
        g_load(n).start()
    greet(1, n_head, False)

    @pl.loop(0, groups)
    def _(g):
        kt[...] = keys[g].T
        acc[...] = jnp.zeros_like(acc)

        @pl.loop(0, n_head)
        def _(c):
            n = g * n_head + c
            q_load(n).wait()
            g_load(n).wait()
            for half in range(chunk // sub):
                start = pl.multiple_of(n * chunk + half * sub, sub)
                rows = pl.ds(start, sub)
                qc, gc = qbuf[rows, :], gbuf[rows, :]
                s = jnp.dot(qc, kt[:lat_width, :], preferred_element_type=f32)
                edge = key_count - LANES
                first = c * span + half * (sub // heads)
                q_pos = first + iota((sub, LANES), 0) // heads
                k_pos = iota((sub, LANES), 1) - (LANES - BLOCK)
                tail = jnp.where(k_pos <= q_pos, s[:, edge:], -jnp.inf)
                s = jnp.concatenate([s[:, :edge], tail], axis=1)
                top = jnp.max(s, axis=1, keepdims=True)
                e = jnp.exp2((s - top) * exp_scale)
                p = e * (1.0 / jnp.sum(e, axis=1, keepdims=True))
                p_low = p.astype(bf16)
                dp = jnp.dot(gc, kt[:val_width, :], preferred_element_type=f32)
                delta = jnp.sum(p * dp, axis=1, keepdims=True)
                ds = (p * (dp - delta) * SCORE_SCALE).astype(bf16)
                dq = jnp.dot(ds, keys[g, :, :lat_width], preferred_element_type=f32)
                dqbuf[rows, :] = dq.astype(bf16)
                both = jnp.concatenate([ds, p_low], axis=0)
                q_t, g_t = qc.T, gc.T
                lhs = jnp.concatenate([q_t[:val_width], g_t], axis=1)
                acc[:val_width, :] += jnp.dot(lhs, both, preferred_element_type=f32)
                acc[val_width:lat_width, :] += jnp.dot(
                    q_t[val_width:], ds, preferred_element_type=f32
                )
                per = sub // heads
                ex[g, c, 0, half * per : (half + 1) * per, :] = jnp.sum(
                    p.reshape(per, heads, key_count), axis=1
                )
            dq_store(n).start()

        @pl.loop(0, BLOCK * idx_heads // sub)
        def _(c):
            start = pl.multiple_of((g * BLOCK * idx_heads) + c * sub, sub)
            rows = pl.ds(start, sub)
            v = jnp.dot(iq[rows, :], kt[640:, :], preferred_element_type=f32) * idx_scale
            logit[rows, :] = v
            silu = v / (1.0 + jnp.exp(-v))
            part = silu * iw[rows, 0:1]
            ex[g, c, 1] = jnp.sum(part.reshape(sub // idx_heads, idx_heads, key_count), axis=1)

        for d in range(1, n_head):
            to = lax.rem(col + d, n_head)
            head_copy(
                ex.at[g, to], exr.at[g, d - 1], ex_send.at[g, d - 1], ex_recv.at[g, d - 1], d, n_head
            ).start()

        for j in range(key_count // LANES):
            part = acc[:, j * LANES : (j + 1) * LANES].astype(bf16).T
            ktb[g, 2 * j : 2 * j + 2] = part.reshape(2, n_head, span, 640)
        for d in range(1, n_head):
            to = lax.rem(col + d, n_head)
            head_copy(
                ktb.at[g, :, to], rsr.at[g, d - 1], rs_send.at[g, d - 1], rs_recv.at[g, d - 1], d, n_head
            ).start()

    @pl.loop(0, groups)
    def _(g):
        for d in range(1, n_head):
            to = lax.rem(col + d, n_head)
            arrival = head_copy(
                ex.at[g, to], exr.at[g, d - 1], ex_send.at[g, d - 1], ex_recv.at[g, d - 1], d, n_head
            )
            arrival.wait_recv()
            arrival.wait_send()
        total = ex[g, col]
        for d in range(1, n_head):
            total = total + exr[g, d - 1]
        target = total[0] * (1.0 / head_total)
        q_pos = col * span + iota((span, key_count), 0)
        k_pos = iota((span, key_count), 1) - (key_count - BLOCK)
        score = jnp.where(k_pos <= q_pos, total[1], -jnp.inf)
        e = jnp.exp(score - jnp.max(score, axis=1, keepdims=True))
        prob = e / jnp.sum(e, axis=1, keepdims=True)
        k_rows = pl.ds(pl.multiple_of(g * BLOCK + col * span, span), span)
        dsb[g, col] = kl[k_rows, 0:1] * (prob - target)
        for d in range(1, n_head):
            head_copy(
                dsb.at[g, col], dsb.at[g, col], ds_send.at[g, d - 1], ds_recv.at[g, d - 1], d, n_head
            ).start()

    @pl.loop(0, groups)
    def _(g):
        for d in range(1, n_head):
            come = lax.rem(col - d + n_head, n_head)
            arrival = head_copy(
                dsb.at[g, col], dsb.at[g, come], ds_send.at[g, d - 1], ds_recv.at[g, d - 1], d, n_head
            )
            arrival.wait_recv()
            arrival.wait_send()
        ik_acc[...] = jnp.zeros_like(ik_acc)

        @pl.loop(0, BLOCK * idx_heads // sub)
        def _(c):
            start = pl.multiple_of((g * BLOCK * idx_heads) + c * sub, sub)
            rows = pl.ds(start, sub)
            v = logit[rows, :]
            sig = 1.0 / (1.0 + jnp.exp(-v))
            d_score = dsb[g, c]
            d_wide = jnp.broadcast_to(
                d_score[:, None, :], (sub // idx_heads, idx_heads, key_count)
            ).reshape(sub, key_count)
            silu = v * sig
            dw[rows, :] = jnp.sum(d_wide * silu, axis=1, keepdims=True)
            slope = sig + silu * (1.0 - sig)
            grad = (d_wide * (iw[rows, 0:1] * idx_scale) * slope).astype(bf16)
            iqc = iq[rows, :]
            diq[rows, :] = jnp.dot(grad, keys[g, :, 640:], preferred_element_type=f32).astype(bf16)
            ik_acc[...] += jnp.dot(iqc.T, grad, preferred_element_type=f32)

        for j in range(key_count // LANES):
            part = ik_acc[:, j * LANES : (j + 1) * LANES].astype(bf16).T
            ikb[g, 2 * j : 2 * j + 2] = part.reshape(2, n_head, span, LANES)
        for d in range(1, n_head):
            to = lax.rem(col + d, n_head)
            head_copy(
                ikb.at[g, :, to], ikr.at[g, d - 1], ik_send.at[g, d - 1], ik_recv.at[g, d - 1], d, n_head
            ).start()

    picks = key_count // BLOCK

    @pl.loop(0, groups)
    def _(g):
        for d in range(1, n_head):
            to = lax.rem(col + d, n_head)
            for arrival in (
                head_copy(
                    ktb.at[g, :, to], rsr.at[g, d - 1], rs_send.at[g, d - 1], rs_recv.at[g, d - 1], d, n_head
                ),
                head_copy(
                    ikb.at[g, :, to], ikr.at[g, d - 1], ik_send.at[g, d - 1], ik_recv.at[g, d - 1], d, n_head
                ),
            ):
                arrival.wait_recv()
                arrival.wait_send()
        lat_sum = ktb[g, :, col].astype(f32)
        key_sum = ikb[g, :, col].astype(f32)
        for d in range(1, n_head):
            lat_sum = lat_sum + rsr[g, d - 1].astype(f32)
            key_sum = key_sum + ikr[g, d - 1].astype(f32)
        tq[g, :, :640] = lat_sum.astype(bf16).reshape(picks * span, 640)
        tq[g, :, 640:] = key_sum.astype(bf16).reshape(picks * span, LANES)

    for n in range(groups * n_head):
        dq_store(n).wait()


def return_kernel(
    n_ctx, n_head, tq, have, ids, out,
    sel, slots, recv, own, a_send, a_recv, x_send, x_recv,
):
    me, col = lax.axis_index("ctx"), lax.axis_index("head")
    blocks, _, quarter, width = out.shape
    rows_in = tq.shape[0]
    per = 256 // (SLOTS * quarter)
    greet(n_ctx, n_head, True)

    @pl.loop(0, n_ctx // per)
    def _(i):
        start = pl.multiple_of(i * 256, 256)
        pick = one_hot(have[pl.ds(start, 256), :], rows_in)
        rows = jnp.dot(pick, tq[...], preferred_element_type=f32).astype(bf16)
        slots[pl.ds(i * per, per)] = rows.reshape(per, SLOTS * quarter, width)

    exchange_ctx(slots, recv, a_send, a_recv, n_ctx)
    recv[me] = slots[me]
    slot_rows(ids, sel, n_ctx, quarter)
    finish_ctx(slots, recv, a_send, a_recv, n_ctx)

    pick = one_hot(sel[...], blocks * quarter)
    total = lax.dot_general(
        pick,
        recv[...].reshape(n_ctx * SLOTS * quarter, width),
        (((0,), (0,)), ((), ())),
        preferred_element_type=f32,
    )
    own[...] = total.astype(bf16).reshape(blocks, quarter, width)

    for d in range(1, n_head):
        head_copy(own, out.at[:, col], x_send.at[d], x_recv.at[d], d, n_head).start()
    out[:, col] = own[...]
    for d in range(1, n_head):
        come = lax.rem(col - d + n_head, n_head)
        arrival = head_copy(own, out.at[:, come], x_send.at[d], x_recv.at[d], d, n_head)
        arrival.wait_recv()
        arrival.wait_send()


VM = pl.BlockSpec(memory_space=pltpu.VMEM)
HB = pl.BlockSpec(memory_space=pl.ANY)
DMA = pltpu.SemaphoreType.DMA


def call(kernel, name, cid, ins, outs, scratch, flops=0):
    return pl.pallas_call(
        kernel,
        name=name,
        in_specs=[spec for spec, _ in ins],
        out_specs=[spec for spec, _ in outs],
        out_shape=[shape for _, shape in outs],
        scratch_shapes=scratch,
        compiler_params=pltpu.CompilerParams(
            collective_id=cid, has_side_effects=True, vmem_limit_bytes=60 * 2**20
        ),
    )(*[value for _, value in ins])


def shards(
    n_ctx, n_head,
    query_latent, d_out, latent, index_query, index_weight, index_key, kl_scale, history, diag_block,
):
    q_dev, heads, lat_width = query_latent.shape
    val_width = d_out.shape[2]
    idx_heads, idx_width = index_query.shape[1:]
    groups, hist = history.shape
    picks = hist + 2
    entries = groups * picks
    key_count = picks * BLOCK
    blk_dev = latent.shape[0] // BLOCK
    quarter = BLOCK // n_head
    slot_total = n_ctx * SLOTS
    width = 768
    shape = jax.ShapeDtypeStruct

    sink = jnp.zeros((groups, 1), i32)
    lists = jnp.concatenate([sink, history, diag_block[:, None]], axis=1).reshape(-1)
    owner, local = lists // blk_dev, lists % blk_dev
    order = jnp.arange(entries)
    earlier = (order[None, :] < order[:, None]) & (owner[None, :] == owner[:, None])
    slot = owner * SLOTS + jnp.sum(earlier.astype(i32), axis=1)
    hits = slot[None, :] == jnp.arange(slot_total)[:, None]
    ask = jnp.sum(jnp.where(hits, local[None, :] + 1, 0), axis=1) - 1
    entry = jnp.sum(jnp.where(hits, order[None, :] + 1, 0), axis=1) - 1
    ask = jnp.pad(ask.reshape(n_ctx, SLOTS), ((0, 0), (0, 8 - SLOTS)), constant_values=-1)
    ask = jnp.broadcast_to(ask[:, :, None], (n_ctx, 8, LANES))

    def lane_rows(ids):
        rows = ids[:, None] * quarter + jnp.arange(quarter)[None, :]
        return jnp.broadcast_to(rows.reshape(-1, 1), (ids.shape[0] * quarter, LANES))

    want, have = lane_rows(slot), lane_rows(entry)

    k_all, ids = call(
        partial(gather_kernel, n_ctx, n_head), "gather_keys", 0,
        [
            (VM, ask), (VM, want),
            (HB, latent.reshape(blk_dev, BLOCK, lat_width)),
            (HB, index_key.reshape(blk_dev, BLOCK, idx_width)),
        ],
        [(VM, shape((entries, n_head, quarter, width), bf16)), (VM, shape((n_ctx, 8, LANES), i32))],
        [
            pltpu.VMEM((blk_dev, quarter, lat_width), bf16),
            pltpu.VMEM((blk_dev, quarter, idx_width), bf16),
            pltpu.VMEM((slot_total * quarter, LANES), i32),
            pltpu.VMEM((n_ctx, SLOTS * quarter, width), bf16),
            pltpu.VMEM((n_ctx, SLOTS * quarter, width), bf16),
            pltpu.VMEM((entries, quarter, width), bf16),
            DMA((2,)), DMA((n_ctx,)), DMA((n_ctx,)), DMA((n_ctx,)), DMA((n_ctx,)),
            DMA((n_head,)), DMA((n_head,)),
        ],
    )

    q_rows, i_rows = q_dev * heads, q_dev * idx_heads
    loads = groups * n_head
    iw = jnp.broadcast_to(index_weight.reshape(i_rows, 1), (i_rows, LANES))
    kl = jnp.broadcast_to(kl_scale[:, None], (q_dev, LANES))
    d_query, d_iq, d_weight, terms = call(
        partial(main_kernel, n_head, heads * n_head), "attend", 1,
        [
            (HB, query_latent.reshape(q_rows, lat_width)),
            (HB, d_out.reshape(q_rows, val_width)),
            (VM, k_all.reshape(groups, key_count, width)),
            (VM, index_query.reshape(i_rows, idx_width)),
            (VM, iw), (VM, kl),
        ],
        [
            (HB, shape((q_rows, lat_width), bf16)),
            (VM, shape((i_rows, idx_width), bf16)),
            (VM, shape((i_rows, 1), f32)),
            (VM, shape((groups, picks * quarter, width), bf16)),
        ],
        [
            pltpu.VMEM((q_rows, lat_width), bf16),
            pltpu.VMEM((q_rows, val_width), bf16),
            pltpu.VMEM((q_rows, lat_width), bf16),
            pltpu.VMEM((width, key_count), bf16),
            pltpu.VMEM((640, key_count), f32),
            pltpu.VMEM((idx_width, key_count), f32),
            pltpu.VMEM((i_rows, key_count), f32),
            pltpu.VMEM((groups, n_head, 2, quarter, key_count), f32),
            pltpu.VMEM((groups, n_head - 1, 2, quarter, key_count), f32),
            pltpu.VMEM((groups, n_head, quarter, key_count), f32),
            pltpu.VMEM((groups, picks, n_head, quarter, 640), bf16),
            pltpu.VMEM((groups, n_head - 1, picks, quarter, 640), bf16),
            pltpu.VMEM((groups, picks, n_head, quarter, idx_width), bf16),
            pltpu.VMEM((groups, n_head - 1, picks, quarter, idx_width), bf16),
            DMA((loads,)), DMA((loads,)), DMA((loads,)),
            DMA((groups, n_head - 1)), DMA((groups, n_head - 1)),
            DMA((groups, n_head - 1)), DMA((groups, n_head - 1)),
            DMA((groups, n_head - 1)), DMA((groups, n_head - 1)),
            DMA((groups, n_head - 1)), DMA((groups, n_head - 1)),
        ],
    )

    (back,) = call(
        partial(return_kernel, n_ctx, n_head), "return_terms", 2,
        [(VM, terms.reshape(entries * quarter, width)), (VM, have), (VM, ids)],
        [(VM, shape((blk_dev, n_head, quarter, width), bf16))],
        [
            pltpu.VMEM((slot_total * quarter, LANES), i32),
            pltpu.VMEM((n_ctx, SLOTS * quarter, width), bf16),
            pltpu.VMEM((n_ctx, SLOTS * quarter, width), bf16),
            pltpu.VMEM((blk_dev, quarter, width), bf16),
            DMA((n_ctx,)), DMA((n_ctx,)), DMA((n_head,)), DMA((n_head,)),
        ],
    )
    back = back.reshape(blk_dev * BLOCK, width)
    return (
        d_query.reshape(q_dev, heads, lat_width),
        back[:, :lat_width],
        d_iq.reshape(q_dev, idx_heads, idx_width),
        d_weight.reshape(q_dev, idx_heads),
        back[:, 640:],
    )


def solution(mesh):
    in_specs = (
        P("ctx", "head", None),
        P("ctx", "head", None),
        P("ctx", None),
        P("ctx", "head", None),
        P("ctx", "head"),
        P("ctx", None),
        P("ctx"),
        P("ctx", None),
        P("ctx"),
    )
    out_specs = (
        P("ctx", "head", None),
        P("ctx", None),
        P("ctx", "head", None),
        P("ctx", "head"),
        P("ctx", None),
    )
    body = partial(shards, mesh.shape["ctx"], mesh.shape["head"])
    return jax.shard_map(body, mesh=mesh, in_specs=in_specs, out_specs=out_specs, check_vma=False)
```

time: 667 us -> 277 us (0.42)
  waiting for transfers between devices: 251 us -> 0 us
  Pallas kernels: 0 us -> 236 us
  blocking collectives: 125 us -> 0 us
  other arithmetic: 106 us -> 1.54 us
  matrix products: 43.3 us -> 0 us
  local copies, waits for them, and re-layouts: 76.8 us -> 35.7 us
  starting transfers between devices: 32.3 us -> 0 us
  between operations: 14.6 us -> 0.74 us
  loops' own time: 13 us -> 0 us
    pallas_call x0 -> x3, Pallas kernels: none -> 236 us  [call(): pl.pallas_call(kernel, name=name, in_specs=[spec for spec, _ in ins], out...]
    all_to_all x4 -> x0, waiting for transfers between devices: 205 us -> none  [the longest x1 149 us: shards(): lax.all_to_all(grad_slots, 'ctx', split_axis=0, concat_axis=0, tiled=True)]
    psum x1 -> x0, blocking collectives: 112 us -> none  [shards(): owned_lat, owned_key = lax.psum((owned_lat, owned_key), 'head')]
    psum x1 -> x0, waiting for transfers between devices: 45.8 us -> none  [shards(): prob_total, score_total = lax.psum((prob_sum, score_part), 'head')]
    scatter-add x4 -> x0, other arithmetic: 44.7 us -> none  [the longest x1 21.2 us: shards(): owned_lat = jnp.zeros((blk_dev, block_size, full_width), jnp.float32).at[...]
    dot_general x16 -> x0, matrix products: 43.3 us -> none  [the longest x2 8.46 us: main_block(): jnp.einsum('rd,td->rt', q_flat, lat_keys, preferred_element_type=jnp.floa...]
    all_to_all x4 -> x0, starting transfers between devices: 32.2 us -> none  [the longest x1 9.34 us: shards(): lax.all_to_all(grad_slots, 'ctx', split_axis=0, concat_axis=0, tiled=True)]
    reduce_sum x10 -> x2, other arithmetic: 30.7 us -> 0.28 us  [the longest x1 0.18 us: shards(): slot = owner * SLOTS + jnp.sum(earlier.astype(i32), axis=1)]
  transfers between devices with their start and end apart: 5 -> 0, of which waited for: 5 -> 0; matrix products, arithmetic and copies ran while one was open for 10% -> 0% of each run, Pallas kernels for 0% -> 0%
where the time goes in v1:
time: 277 us; the launch traced here: 274 us
  Pallas kernels  236 us (85%)
  local copies, waits for them, and re-layouts  35.7 us (13%)
    pallas_call x3, Pallas kernels, call(): pl.pallas_call(kernel, name=name, in_specs=[spec for spec, _ in ins], out...  236 us
    unnamed x15, local copies, waits for them, and re-layouts  26 us

profile of v1, /device:TPU:48, one launch (start us, length us, event | category | flops | bytes accessed | tf_op | source)
XLA Modules:
  0.0 273.8 jit_solution(5985869868880320878)
XLA Ops:
  0.6 0.7 copy.28
  1.4 0.8 pad_add_fusion
  2.1 0.1 reshape.203
  2.2 0.2 convert_reduce_fusion
  2.4 0.1 select_reduce_fusion
  2.5 0.1 sub.16
  2.7 0.8 broadcast_in_dim.35.ask
  3.4 0.1 iota_add_fusion.1
  3.5 0.1 add.108
  3.6 0.8 broadcast_in_dim.36.want
  4.4 4.3 %copy.29 = bf16[2048,576]{1,0:T(8,128)(2,1)} copy(bf16[2048,576]{0,1:T(8,128)(2,1)} %param.11) | data formatting | bytes 4718592 | tf_op args[2]
  8.7 81.2 %gather_keys.1 = (bf16[32,4,16,768]{3,2,1,0:T(8,128)(2,1)}, s32[32,8,128]{2,1,0:T(8,128)}) custom-call(s32[32,8,128]{2,1,0:T(8,128)} %broadcast_in_dim.35.ask, s32[512,128]{1,0:T(8,128)} %broadcast_in_dim.36.want, bf16[32,64,576]{2,1,0:T(8,128)(2,1)} %bitcast.15, bf16[32,64,128]{2,1,0:T(8,128)(2,1)} %bitcast.21), custom_call_target="tpu_custom_call" | custom-call | tf_op jit(solution)/shard_map/gather_keys/pallas_call | solution.py:415
  89.9 0.0 copy-start.2
  89.9 0.0 copy-start.3
  89.9 8.9 %copy.27 = bf16[128,32,576]{2,1,0:T(8,128)(2,1)} copy(bf16[128,32,576]{0,2,1:T(8,128)(2,1)} %param.9) | data formatting | bytes 9437184 | tf_op args[0]
  98.8 0.1 copy.30
  98.9 0.1 broadcast_in_dim.37
  99.0 1.3 broadcast_in_dim.68.iw
  100.3 0.7 broadcast_in_dim.69.kl
  101.0 83.9 %attend.1 = (bf16[4096,576]{1,0:T(8,128)(2,1)}, bf16[2048,128]{1,0:T(8,128)(2,1)}, f32[2048,1]{1,0:T(8,128)}, bf16[2,256,768]{2,1,0:T(8,128)(2,1)}) custom-call(bf16[4096,576]{1,0:T(8,128)(2,1)} %bitcast.12, bf16[4096,512]{1,0:T(8,128)(2,1)} %bitcast.17, bf16[2,1024,768]{2,1,0:T(8,128)(2,1)} %bitcast.18, bf16[2048,128]{1,0:T(8,128)(2,1)} %bitcast.20, ...), custom_call_target="tpu_custom_call" | custom-call | tf_op jit(solution)/shard_map/attend/pallas_call | solution.py:415
  184.9 0.1 iota_add_fusion
  185.0 0.1 add.113
  185.0 1.0 broadcast_in_dim.71.have
  186.0 70.7 %return_terms.1 = bf16[32,4,16,768]{3,2,1,0:T(8,128)(2,1)} custom-call(bf16[512,768]{1,0:T(8,128)(2,1)} %bitcast.19, s32[1024,128]{1,0:T(8,128)} %broadcast_in_dim.71.have, s32[32,8,128]{2,1,0:T(8,128)} %get-tuple-element.14.ids), custom_call_target="tpu_custom_call" | custom-call | tf_op jit(solution)/shard_map/return_terms/pallas_call | solution.py:415
  256.8 2.0 slice.8
  258.7 2.5 copy.32
  261.3 1.9 slice.9
  263.1 8.7 %copy.31 = bf16[128,32,576]{0,2,1:T(8,128)(2,1)} copy(bf16[128,32,576]{2,1,0:T(8,128)(2,1)} %bitcast.16) | data formatting | bytes 9437184
  271.9 0.3 reduce
  272.2 0.1 reshape.212
  272.3 0.7 copy.33
  273.0 0.8 copy.35
  (12 shorter events, 0.1 us)
Async XLA Ops:
  89.9 8.9 %copy-start.2 = (f32[128,16]{0,1:T(8,128)S(1)}, f32[128,16]{0,1:T(8,128)}, u32[]{:S(2)}) copy-start(f32[128,16]{0,1:T(8,128)} %param.13) | copy-start | bytes 24580
  89.9 10.4 %copy-start.3 = (f32[128]{0:T(128)S(1)}, f32[128]{0:T(128)}, u32[]{:S(2)}) copy-start(f32[128]{0:T(128)} %param.15) | copy-start | bytes 1540
  263.1 8.7 %copy-start = (f32[2048,1]{1,0:T(8,128)S(1)}, f32[2048,1]{1,0:T(8,128)}, u32[]{:S(2)}) copy-start(f32[2048,1]{1,0:T(8,128)} %get-tuple-element.16) | copy-start | bytes 24580
  263.1 9.8 %copy-start.1 = (bf16[2048,128]{1,0:T(8,128)(2,1)S(1)}, bf16[2048,128]{1,0:T(8,128)(2,1)}, u32[]{:S(2)}) copy-start(bf16[2048,128]{1,0:T(8,128)(2,1)} %get-tuple-element.15) | copy-start | bytes 1572868
